TPU v7x, 512 devices: a whole 4x8x8 slice. The times are simulated.
512 devices in a mesh: blk: 8 (over y_hi, core), group: 64 (over z, y_lo, x).
Axes of the slice: x: 4, y: 8 (y_hi: 4, y_lo: 2; y = y_hi * 2 + y_lo), z: 8, core: 2. Of those that a mesh axis runs over, the one named last changes fastest.
Arguments:
- query_states: bfloat16 [36864, 4096], P(('blk', 'group')), may hold values from -6 to 6
- passage_states: bfloat16 [36864, 4096], P(('blk', 'group')), may hold values from -6 to 6
- norm_gain: float32 [4096], replicated, may hold values from 0.5 to 1.5
- negative_owner: int32 [36864, 4], P(('blk', 'group')), may hold values from 0 to 63, all different within a row; in each aligned block of 72 rows (0 to 71, 72 to 143, ...) at most 5 rows name the same one
- negative_row: int32 [36864, 4], P(('blk', 'group')), may hold values from 0 to 71
Outputs:
- query_grad: float32 [36864, 4096], P(('blk', 'group'))
- passage_grad: float32 [36864, 4096], P(('blk', 'group'))
- gain_grad: float32 [4096], replicated
- loss: float32 [], replicated
Inputs may be any that keep to these rules, and one draw needn't show every extreme that they name: `negative_owner`: the 4 owners of one query are distinct. Among the rows of one device, no owner is named by more than 5 rows.
All inputs are finite; a program needn't handle non-finite values.
Results may differ from a plain program's by a relative error of at most 0.0018.
The roundings to bfloat16 on the way count: a program that leaves them out, or rounds other values in their place, can miss the bound.
Values may be sent and summed in bfloat16 or wider, within the bound.
A program may use at most 64 MiB of HBM per device.

v0:
```python
import math

import jax
import jax.numpy as jnp
from jax import lax
from jax.sharding import PartitionSpec as P

EPSILON = 1e-05


def embed_rows(states, gain_vector):
    values = states.astype(jnp.float32)
    inverse = lax.rsqrt(jnp.mean(values * values, axis=-1, keepdims=True) + EPSILON)
    return ((values * inverse * gain_vector).astype(jnp.bfloat16), inverse)


def norm_backward(states, inverse, gain_vector, upstream):
    values = states.astype(jnp.float32)
    scaled = gain_vector * upstream
    inner_sum = jnp.sum(scaled * values, axis=-1, keepdims=True)
    grad_states = scaled * inverse - values * inverse**3 * inner_sum / values.shape[-1]
    grad_gain = jnp.sum(upstream * values * inverse, axis=0)
    return (grad_states, grad_gain)


def local(query_states, passage_states, norm_gain, negative_owner, negative_row):
    batch_dev, width = query_states.shape
    negatives = negative_owner.shape[1]
    groups = lax.axis_size("group")
    blocks = lax.axis_size("blk")
    capacity = max(2, 5 * batch_dev * negatives // (4 * groups))
    score_scale = 4.0 / math.sqrt(width)
    query_embed, query_inverse = embed_rows(query_states, norm_gain)
    passage_embed, passage_inverse = embed_rows(passage_states, norm_gain)
    entries = batch_dev * negatives
    owner_flat = negative_owner.reshape(entries)
    row_flat = negative_row.reshape(entries)
    owner_match = (owner_flat[:, None] == jnp.arange(groups, dtype=jnp.int32)[None, :]).astype(
        jnp.int32
    )
    earlier = jnp.cumsum(owner_match, axis=0) - owner_match
    slot_rank = jnp.sum(earlier * owner_match, axis=1)
    slot_index = owner_flat * capacity + slot_rank
    request = (
        jnp.zeros((groups * capacity,), jnp.int32)
        .at[slot_index]
        .set(row_flat)
        .reshape(groups, capacity)
    )
    slot_live = jnp.zeros((groups * capacity,), jnp.bool_).at[slot_index].set(True)
    wanted = lax.all_to_all(request, "group", split_axis=0, concat_axis=0, tiled=True)
    found_rows = jnp.take(passage_embed, wanted, axis=0)
    returned = lax.all_to_all(found_rows, "group", split_axis=0, concat_axis=0, tiled=True)
    pool_rows = returned.reshape(groups * capacity, width)
    pool_scores = (
        jnp.einsum("qd,pd->qp", query_embed, pool_rows, preferred_element_type=jnp.float32)
        * score_scale
    )
    pool_masked = jnp.where(slot_live[None, :], pool_scores, -jnp.inf)
    my_blk = lax.axis_index("blk")
    columns = jnp.arange(blocks * batch_dev, dtype=jnp.int32)
    positive_col = my_blk * batch_dev + jnp.arange(batch_dev, dtype=jnp.int32)
    target = (columns[None, :] == positive_col[:, None]).astype(jnp.float32)
    all_passages = lax.all_gather(passage_embed, "blk", axis=0, tiled=True)
    batch_scores = (
        jnp.einsum("qd,pd->qp", query_embed, all_passages, preferred_element_type=jnp.float32)
        * score_scale
    )
    row_peak = jnp.maximum(jnp.max(batch_scores, axis=1), jnp.max(pool_masked, axis=1))[:, None]
    summed = (
        jnp.sum(jnp.exp(batch_scores - row_peak), axis=1)
        + jnp.sum(jnp.where(slot_live[None, :], jnp.exp(pool_masked - row_peak), 0.0), axis=1)
    )[:, None]
    row_totals = row_peak + jnp.log(summed)
    all_queries = lax.all_gather(query_embed, "blk", axis=0, tiled=True)
    all_totals = lax.all_gather(row_totals, "blk", axis=0, tiled=True)
    owner_scores = (
        jnp.einsum("qd,pd->qp", all_queries, passage_embed, preferred_element_type=jnp.float32)
        * score_scale
    )
    coefficient = (jnp.exp(owner_scores - all_totals) - target.T).astype(jnp.bfloat16)
    batch_grad = score_scale * jnp.einsum(
        "qp,qd->pd", coefficient, all_queries, preferred_element_type=jnp.float32
    )
    batch_coefficient = (jnp.exp(batch_scores - row_totals) - target).astype(jnp.bfloat16)
    pool_coefficient = jnp.where(slot_live[None, :], jnp.exp(pool_masked - row_totals), 0.0).astype(
        jnp.bfloat16
    )
    query_embed_grad = score_scale * (
        jnp.dot(batch_coefficient, all_passages, preferred_element_type=jnp.float32)
        + jnp.dot(pool_coefficient, pool_rows, preferred_element_type=jnp.float32)
    )
    pool_terms = (
        score_scale
        * jnp.einsum("qp,qd->pd", pool_coefficient, query_embed, preferred_element_type=jnp.float32)
    ).astype(jnp.bfloat16)
    returned_terms = lax.all_to_all(
        pool_terms.reshape(groups, capacity, width),
        "group",
        split_axis=0,
        concat_axis=0,
        tiled=True,
    )
    flat_terms = returned_terms.reshape(groups * capacity, width)
    served_flat = wanted.reshape(groups * capacity)
    placement_table = (
        jnp.arange(batch_dev, dtype=jnp.int32)[:, None] == served_flat[None, :]
    ).astype(jnp.bfloat16)
    passage_embed_grad = batch_grad + jnp.dot(
        placement_table, flat_terms, preferred_element_type=jnp.float32
    )
    positive_score = jnp.sum(batch_scores * target, axis=1)
    loss_part = jnp.sum(row_totals[:, 0] - positive_score)
    query_grad, gain_query = norm_backward(query_states, query_inverse, norm_gain, query_embed_grad)
    passage_grad, gain_passage = norm_backward(
        passage_states, passage_inverse, norm_gain, passage_embed_grad
    )
    gain_grad, loss_sum = lax.psum((gain_query + gain_passage, loss_part), ("blk", "group"))
    loss = loss_sum / (batch_dev * blocks * groups)
    return (query_grad, passage_grad, gain_grad, loss)


def solution(mesh):
    return jax.shard_map(
        local,
        mesh=mesh,
        in_specs=(
            P(("blk", "group"), None),
            P(("blk", "group"), None),
            P(),
            P(("blk", "group"), None),
            P(("blk", "group"), None),
        ),
        out_specs=(P(("blk", "group"), None), P(("blk", "group"), None), P(), P()),
        check_vma=False,
    )
```

profile of v0, /device:TPU:1, one launch (start us, length us, event | category | flops | bytes accessed | tf_op | source)
XLA Modules:
  0.0 409.0 jit_solution(2207086108578834446)
XLA Ops:
  7.2 1.4 fusion.10
  8.6 1.3 fusion.1
  10.5 2.1 fusion.3
  13.1 0.9 reduce-window.6
  14.7 2.9 scatter_custom_fusion.1
  17.7 24.4 %all_to_all.25 = s32[64,1,5]{2,1,0:T(1,128)S(1)} all-to-all(s32[64,1,5]{2,1,0:T(1,128)S(1)} %bitcast.32), channel_id=1, replica_groups=mesh['blk'=8,'group'=64] {'group'}, dimensions={0} | all-to-all | bytes 2560 | tf_op jit(solution)/shard_map/all_to_all | solution.py:51
  42.3 3.3 gather_fusion
  45.6 2.8 reshape.183
  48.4 4.7 %broadcast_select_fusion = bf16[64,5,4096]{2,1,0:T(8,128)(2,1)} fusion(bf16[64,5,4096]{2,1,0:T(8,128)(2,1)} %reshape.183, pred[64,5]{1,0:T(8,128)(4,1)S(1)} %compare_and_fusion), kind=kLoop, calls=%fused_computation.8 | loop fusion | flops 1310720 | bytes 5243200 | tf_op jit(solution)/shard_map/jit(_take)/select_n | solution.py:52
  53.1 5.7 %all-to-all-start.1 = ((bf16[64,5,4096]{2,1,0:T(8,128)(2,1)}), bf16[64,5,4096]{2,1,0:T(8,128)(2,1)}, u32[]{:S(2)}, u32[]{:S(2)}) async-start(bf16[64,5,4096]{2,1,0:T(8,128)(2,1)} %broadcast_select_fusion), calls=%async_computation.1 | async-start | bytes 8388608 | tf_op jit(solution)/shard_map/all_to_all | solution.py:53
  59.6 1.6 scatter_custom_fusion
  61.2 105.4 %all-to-all-done.1 = bf16[64,5,4096]{2,1,0:T(8,128)(2,1)} async-done(((bf16[64,5,4096]{2,1,0:T(8,128)(2,1)}), bf16[64,5,4096]{2,1,0:T(8,128)(2,1)}, u32[]{:S(2)}, u32[]{:S(2)}) %all-to-all-start.1) | async-done | bytes 2621472 | tf_op jit(solution)/shard_map/all_to_all | solution.py:53
  166.6 3.4 reshape.178
  170.0 2.1 fusion.41
  172.1 4.2 %fusion.40 = (f32[72]{0:T(128)S(1)}, f32[72,576]{1,0:T(8,128)S(1)}) fusion(bf16[72,4096]{1,0:T(8,128)(2,1)} %get-tuple-element.14, bf16[576,4096]{1,0:T(8,128)(2,1)} %all-gather.4.cloned.1.call-done), kind=kOutput, calls=%fused_computation.91 | convolution fusion | flops 339821504 | bytes 5474592 | tf_op jit(solution)/shard_map/qd,pd->qp/dot_general | solution.py:66
  177.9 2.4 fusion
  180.4 4.8 %reshape.179 = bf16[64,5,4096]{2,1,0:T(8,128)(2,1)} reshape(bf16[320,4096]{1,0:T(8,128)(2,1)} %fusion) | data formatting | bytes 5242880 | tf_op jit(solution)/shard_map/reshape | solution.py:98
  185.2 12.5 %all-to-all-start.2 = ((bf16[64,5,4096]{2,1,0:T(8,128)(2,1)}), bf16[64,5,4096]{2,1,0:T(8,128)(2,1)}, u32[]{:S(2)}, u32[]{:S(2)}) async-start(bf16[64,5,4096]{2,1,0:T(8,128)(2,1)} %reshape.179), calls=%async_computation.2 | async-start | bytes 8388608 | tf_op jit(solution)/shard_map/all_to_all | solution.py:97
  197.7 1.3 dynamic-slice
  200.8 1.4 reduce.7
  202.2 1.5 eq.71
  203.7 0.8 dynamic-update-slice
  204.5 62.5 %all-reduce.1 = f32[576]{0:T(1024)} all-reduce(f32[576]{0:T(1024)S(1)} %dynamic-update-slice), channel_id=2, replica_groups=mesh['blk'=8,'group'=64] {'blk'}, use_global_device_ids=true, to_apply=%add.1 | all-reduce | flops 576 | bytes 4608
  267.0 3.5 fusion.27
  270.5 2.1 fusion.9
  272.7 7.7 %convolution_multiply_fusion.1 = f32[72,4096]{1,0:T(8,128)} fusion(bf16[576,4096]{1,0:T(8,128)(2,1)} %all-gather.6.cloned.1.call-done, bf16[72,4096]{1,0:T(8,128)(2,1)S(1)} %copy-done, f32[576]{0:T(1024)S(1)} %copy-done.12, s32[72]{0:T(128)S(1)} %copy-done.23), kind=kOutput, calls=%fused_computation.6 | convolution fusion | flops 680020992 | bytes 6490656 | tf_op jit(solution)/shard_map/qp,qd->pd/dot_general | solution.py:82
  280.4 1.3 fusion.6
  281.7 9.2 %all-to-all-done.2 = bf16[64,5,4096]{2,1,0:T(8,128)(2,1)} async-done(((bf16[64,5,4096]{2,1,0:T(8,128)(2,1)}), bf16[64,5,4096]{2,1,0:T(8,128)(2,1)}, u32[]{:S(2)}, u32[]{:S(2)}) %all-to-all-start.2) | async-done | bytes 2621472 | tf_op jit(solution)/shard_map/all_to_all | solution.py:97
  290.9 3.4 reshape.180
  294.4 3.3 fusion.18
  297.7 100.1 %all-reduce.2 = (f32[4096]{0:T(1024)}, f32[]{:T(128)}) all-reduce(f32[4096]{0:T(1024)S(1)} %add.131, f32[]{:T(128)} %get-tuple-element.12), channel_id=1, replica_groups=mesh['blk'=8,'group'=64] {'blk','group'}, use_global_device_ids=true, to_apply=%region_15.16 | all-reduce | flops 4097 | bytes 32776 | tf_op jit(solution)/shard_map/psum | solution.py:118
  398.4 2.6 fusion.15
  (90 shorter events, 5.7 us)
Async XLA Ops:
  7.2 3.3 copy-start.5
  7.2 3.3 copy-start.2
  7.2 164.9 %all-gather.4.cloned.1.call-start = ((), (), s32[]{:S(2)}) async-start(), calls=%async_computation.3 | async-start | bytes 5308416 | tf_op jit(solution)/shard_map/all_gather | solution.py:64
  10.5 2.1 copy-start.15
  10.5 2.1 copy-start.17
  10.5 2.2 copy-start.21
  12.6 1.7 copy-start.26
  12.6 29.7 %copy-start = (bf16[72,4096]{1,0:T(8,128)(2,1)S(1)}, bf16[72,4096]{1,0:T(8,128)(2,1)}, u32[]{:S(2)}) copy-start(bf16[72,4096]{1,0:T(8,128)(2,1)} %get-tuple-element.15) | copy-start | bytes 1769476
  53.1 113.5 %all-to-all-start.1 = ((bf16[64,5,4096]{2,1,0:T(8,128)(2,1)}), bf16[64,5,4096]{2,1,0:T(8,128)(2,1)}, u32[]{:S(2)}, u32[]{:S(2)}) async-start(bf16[64,5,4096]{2,1,0:T(8,128)(2,1)} %broadcast_select_fusion), calls=%async_computation.1 | async-start | bytes 8388608 | tf_op jit(solution)/shard_map/all_to_all | solution.py:53
  58.8 213.9 %all-gather.6.cloned.1.call-start = ((), (), s32[]{:S(2)}) async-start(), calls=%async_computation.4 | async-start | bytes 5308416 | tf_op jit(solution)/shard_map/all_gather | solution.py:75
  61.2 116.2 %copy-start.10 = (pred[320]{0:T(512)(128)(4,1)}, pred[320]{0:T(512)(128)(4,1)S(1)}, u32[]{:S(2)}) copy-start(pred[320]{0:T(512)(128)(4,1)S(1)} %scatter_custom_fusion) | copy-start | bytes 964
  61.2 115.4 %copy-start.22 = (s32[72]{0:T(128)}, s32[72]{0:T(128)S(1)}, u32[]{:S(2)}) copy-start(s32[72]{0:T(128)S(1)} %iota_add_fusion) | copy-start | bytes 868
  172.1 5.8 %copy-start.1 = (bf16[72,4096]{1,0:T(8,128)(2,1)S(1)}, bf16[72,4096]{1,0:T(8,128)(2,1)}, u32[]{:S(2)}) copy-start(bf16[72,4096]{1,0:T(8,128)(2,1)} %get-tuple-element.14) | copy-start | bytes 1769476
  177.4 0.5 copy-start.13
  185.2 14.4 %copy-start.8 = (f32[4096]{0:T(1024)S(1)}, f32[4096]{0:T(1024)}, u32[]{:S(2)}) copy-start(f32[4096]{0:T(1024)} %param.7) | copy-start | bytes 49156
  185.2 105.8 %all-to-all-start.2 = ((bf16[64,5,4096]{2,1,0:T(8,128)(2,1)}), bf16[64,5,4096]{2,1,0:T(8,128)(2,1)}, u32[]{:S(2)}, u32[]{:S(2)}) async-start(bf16[64,5,4096]{2,1,0:T(8,128)(2,1)} %reshape.179), calls=%async_computation.2 | async-start | bytes 8388608 | tf_op jit(solution)/shard_map/all_to_all | solution.py:97
  266.9 3.5 copy-start.3
  266.9 3.5 copy-start.9
  266.9 3.5 copy-start.11
  266.9 3.5 copy-start.14
  266.9 3.5 copy-start.18
  270.5 2.2 copy-start.12
  270.5 2.2 copy-start.23
  272.6 7.7 %copy-start.4 = (bf16[72,4096]{1,0:T(8,128)(2,1)S(1)}, bf16[72,4096]{1,0:T(8,128)(2,1)}, u32[]{:S(2)}) copy-start(bf16[72,4096]{1,0:T(8,128)(2,1)} %param.5) | copy-start | bytes 1769476
  272.6 7.7 %copy-start.7 = (f32[72,4096]{1,0:T(8,128)S(1)}, f32[72,4096]{1,0:T(8,128)}, u32[]{:S(2)}) copy-start(f32[72,4096]{1,0:T(8,128)} %get-tuple-element.24) | copy-start | bytes 3538948
  272.7 7.7 %copy-start.19 = (f32[72]{0:T(128)S(1)}, f32[72]{0:T(128)}, u32[]{:S(2)}) copy-start(f32[72]{0:T(128)} %copy-done.17) | copy-start | bytes 868
  272.7 7.7 %copy-start.25 = (f32[72]{0:T(128)S(1)}, f32[72]{0:T(128)}, u32[]{:S(2)}) copy-start(f32[72]{0:T(128)} %get-tuple-element.27) | copy-start | bytes 868
  281.7 12.6 %copy-start.6 = (bf16[72,4096]{1,0:T(8,128)(2,1)S(1)}, bf16[72,4096]{1,0:T(8,128)(2,1)}, u32[]{:S(2)}) copy-start(bf16[72,4096]{1,0:T(8,128)(2,1)} %param.6) | copy-start | bytes 1769476
  281.7 12.6 %copy-start.16 = (f32[72]{0:T(128)S(1)}, f32[72]{0:T(128)}, u32[]{:S(2)}) copy-start(f32[72]{0:T(128)} %copy-done.15) | copy-start | bytes 868
  281.7 12.6 %copy-start.20 = (s32[320]{0:T(512)S(1)}, s32[320]{0:T(512)}, u32[]{:S(2)}) copy-start(s32[320]{0:T(512)} %eq.71) | copy-start | bytes 3844
  294.4 104.0 %copy-start.24 = (f32[72]{0:T(128)S(1)}, f32[72]{0:T(128)}, u32[]{:S(2)}) copy-start(f32[72]{0:T(128)} %get-tuple-element.16) | copy-start | bytes 868
Sparse Core Ops, SparseCore 0:
  12.8 70.3 all-gather.3
  85.9 80.4 all-gather.5
where the time goes:
time: 410 us; the launch traced here: 409 us
  blocking collectives  187 us (46%)
  waiting for transfers between devices  115 us (28%)
  local copies, waits for them, and re-layouts  28.1 us (7%)
  matrix products  25.3 us (6%)
  starting transfers between devices  18.2 us (4%)
  other arithmetic  18.2 us (4%)
  between operations  17 us (4%)
    all_to_all x1, waiting for transfers between devices, local(): lax.all_to_all(found_rows, 'group', split_axis=0, concat_axis=0, tiled=True)  105 us
    psum x1, blocking collectives, local(): lax.psum((gain_query + gain_passage, loss_part), ('blk', 'group'))  100 us
    unnamed x1, blocking collectives  62.5 us
    all_to_all x1, blocking collectives, local(): lax.all_to_all(request, 'group', split_axis=0, concat_axis=0, tiled=True)  24.4 us
    all_to_all x1, starting transfers between devices, local(): lax.all_to_all(pool_terms.reshape(groups, capacity, width), 'group', spli...  12.5 us
    all_to_all x1, waiting for transfers between devices, local(): lax.all_to_all(pool_terms.reshape(groups, capacity, width), 'group', spli...  9.19 us
  transfers between devices with their start and end apart: 4, of which 2 were waited for; matrix products, arithmetic and copies ran while one was open for 14% of the time, Pallas kernels for 0%

commit v1 on v0

v1 whole, which is shorter than its diff:
```python
import math

import jax
import jax.numpy as jnp
from jax import lax
from jax.experimental import pallas as pl
from jax.experimental.pallas import tpu as pltpu
from jax.sharding import PartitionSpec as P

EPSILON = 1e-05
MESH = pl.DeviceIdType.MESH
NZ, NY, NX = 8, 2, 4
NGROUP = NZ * NY * NX
NPOS, NCORE = 4, 2
NBLK = NPOS * NCORE
ROWS, WIDTH = 72, 4096
PAD = 80
SLOTS = 5
POOL = NGROUP * SLOTS
CHUNKS = NZ // 2
CROWS = POOL // CHUNKS
PLANE = NY * NX
LANES = CHUNKS * 128
FOLD, FOLDW = 16, 256
HEAD, TAILW = 64, 2048
HEADS, TAILS = NBLK * HEAD, NBLK * FOLD
STRIP = 512
SCALE = 4.0 / math.sqrt(WIDTH)
GAINS = WIDTH + 128
VMEM_LIMIT = 60 * 1024 * 1024
BF, F32, I32 = jnp.bfloat16, jnp.float32, jnp.int32


def turn_z(place):
    odd, half = place % 2, place // 2
    return (1 - odd) * half + odd * (NZ - 1 - half)


def peer(me, turn, back=False):
    z, y, x = me // (NY * NX), (me // NX) % NY, me % NX
    dz, dy, dx = turn_z(turn // (NY * NX)), (turn // NX) % NY, turn % NX
    if back:
        dz, dx = NZ - dz, NX - dx
    return (((z + dz) % NZ) * NY + (y + dy) % NY) * NX + (x + dx) % NX


def turn_of(me, other):
    dz = (other // (NY * NX) - me // (NY * NX)) % NZ
    dy = ((other // NX) % NY - (me // NX) % NY) % NY
    dx = (other % NX - me % NX) % NX
    place = jnp.where(dz < NZ // 2, 2 * dz, 2 * (NZ - 1 - dz) + 1)
    return (place * NY + dy) * NX + dx


def remote(src, dst, send, recv, **where):
    return pltpu.make_async_remote_copy(
        src_ref=src, dst_ref=dst, send_sem=send, recv_sem=recv, device_id=where, device_id_type=MESH
    )


class Spread:
    def __init__(self, blk, head, tail, send, recv):
        pos, core = blk // NCORE, blk % NCORE
        self.own = blk
        self.right = ((pos + 1) % NPOS) * NCORE + core
        self.left = ((pos + 3) % NPOS) * NCORE + core
        self.far = ((pos + 2) % NPOS) * NCORE + core
        self.twin = pos * NCORE + 1 - core
        self.head, self.tail, self.send, self.recv = head, tail, send, recv
        self.started = []

    def copy(self, kind, slot, piece, target):
        if piece < 4 and kind in (0, 1, 3, 5):
            ref = self.head.at[slot, pl.ds(piece * FOLD, FOLD)]
        elif piece < 4:
            ref = self.head.at[slot]
        elif kind in (3, 5):
            ref = self.tail.at[slot, :, pl.ds((kind // 5) * (TAILW // 2), TAILW // 2)]
        else:
            ref = self.tail.at[slot]
        sems = self.send.at[kind, piece], self.recv.at[kind, piece]
        return remote(ref, ref, *sems, blk=target)

    def start(self, kind, slot, piece, target):
        copy = self.copy(kind, slot, piece, target)
        copy.start()
        self.started.append(copy)

    def arrived(self, kind, slot, piece):
        self.copy(kind, slot, piece, self.own).wait_recv()

    def hop(self, *pieces):
        for piece in pieces:
            self.start(0, self.own, piece, self.right)
            self.start(1, self.own, (2, 3, 0, 1, 4)[piece], self.left)

    def over(self, kind, slot):
        self.start(kind, slot, 0, self.twin)
        self.start(kind, slot, 4, self.twin)

    def relay(self, *pieces):
        for piece in pieces:
            self.arrived(0, self.left, piece)
            self.start(3, self.left, piece, self.right)
            other = (2, 3, 0, 1, 4)[piece]
            self.arrived(1, self.right, other)
            self.start(5, self.right, other, self.left)

    def pass_near(self):
        self.arrived(0, self.left, 2)
        self.arrived(0, self.left, 3)
        self.over(4, self.left)
        self.arrived(1, self.right, 0)
        self.arrived(1, self.right, 1)
        self.over(6, self.right)

    def pass_far(self):
        for piece in (0, 1, 4):
            self.arrived(3, self.far, piece)
        for piece in (2, 3, 4):
            self.arrived(5, self.far, piece)
        self.over(7, self.far)

    def finish(self):
        for kind in (2, 4, 6, 7):
            self.arrived(kind, self.twin, 0)
            self.arrived(kind, self.twin, 4)

    def sent(self):
        for copy in self.started:
            copy.wait_send()


class Swap:
    def __init__(self, me, src, dst, send, recv, back):
        self.me, self.src, self.dst, self.send, self.recv, self.back = me, src, dst, send, recv, back

    def each(self, chunk, first, count, act):
        @pl.loop(first, first + count)
        def _(plane):
            for side in range(2):
                turn = (2 * chunk + side) * PLANE + plane

                @pl.when(turn > 0)
                def _():
                    rows = pl.ds(turn * SLOTS, SLOTS)
                    act(
                        remote(
                            self.src.at[rows],
                            self.dst.at[rows],
                            self.send.at[turn],
                            self.recv.at[turn],
                            group=peer(self.me, turn, self.back),
                        )
                    )

    def start(self, chunk, half):
        self.each(chunk, half * (PLANE // 2), PLANE // 2, lambda copy: copy.start())

    def arrived(self, chunk):
        self.each(chunk, 0, PLANE, lambda copy: copy.wait_recv())

    def sent(self):
        @pl.loop(0, CHUNKS)
        def _(chunk):
            self.each(chunk, 0, PLANE, lambda copy: copy.wait_send())


def iota(shape, dim):
    return lax.broadcasted_iota(I32, shape, dim)


def rows_of(start, count=FOLD):
    return pl.ds(pl.multiple_of(start, FOLD), count)


def to_column(row, count):
    same = iota((count, 128), 0) == iota((count, 128), 1)
    return jnp.sum(jnp.where(same, jnp.broadcast_to(row, (count, 128)), 0), axis=1, keepdims=True)


def matmul(left, right):
    return jnp.dot(left, right, preferred_element_type=F32)


def matmul_t(left, right):
    return lax.dot_general(left, right, (((1,), (1,)), ((), ())), preferred_element_type=F32)


def embed(states, gain, out, inverses):
    @pl.loop(0, PAD // FOLD)
    def _(step):
        at = rows_of(step * FOLD)
        values = states[at, :].astype(F32)
        inverse = lax.rsqrt(jnp.mean(values * values, axis=-1, keepdims=True) + EPSILON)
        inverses[at, :] = inverse
        out[at, :] = (values * inverse * gain[...]).astype(BF)


def place_own(blk, embedded, head, tail):
    head[blk] = embedded[0:HEAD, :]
    last = embedded[HEAD:PAD, :]
    last = last.astype(F32)[0 : ROWS - HEAD]
    tail[blk] = jnp.concatenate([last[:, :TAILW], last[:, TAILW:]], axis=0).astype(BF)


def fold_rows(left, right, factor, swap, work, stage, flat, chunk):
    first = chunk * CROWS

    @pl.loop(0, FOLD)
    def _(k):
        cols = pl.ds(pl.multiple_of(k * FOLDW, FOLDW), FOLDW)
        found = matmul(left, right[:, cols])
        if factor is not None:
            found = factor * found
        found = found.astype(BF)
        if flat is not None:
            flat[rows_of(first, CROWS), cols] = found
        work[:, rows_of(k * FOLD), :] = found.reshape(CROWS // FOLD, FOLD, FOLDW)

    for g in range(CROWS // FOLD):
        folded = matmul(swap[...], work[g]).astype(BF)
        stage[pl.ds(first + g * FOLD, FOLD)] = folded.reshape(FOLD, FOLD, FOLDW)


def pair_scores(embedded, head, tail):
    main = matmul_t(embedded[...], head[...].reshape(HEADS, WIDTH)) * SCALE
    folded = tail[...].reshape(TAILS, TAILW)
    low = matmul_t(embedded[:, :TAILW], folded)
    high = matmul_t(embedded[:, TAILW:], folded)
    return main, (low + pltpu.roll(high, TAILS - (ROWS - HEAD), 1)) * SCALE


def pair_masks(blk):
    row, lane = iota((PAD, HEADS), 0), iota((PAD, HEADS), 1)
    main = (row < HEAD) & (lane == blk * HEAD + row)
    row, lane = iota((PAD, TAILS), 0), iota((PAD, TAILS), 1)
    valid = (lane // (ROWS - HEAD)) % 2 == 0
    rest = (row >= HEAD) & (row < ROWS) & (lane == blk * FOLD + row - HEAD)
    return main, rest, valid


def pair_grads(main, rest, head, tail, out, extra):
    low = rest.astype(BF)
    high = pltpu.roll(rest, ROWS - HEAD, 1).astype(BF)
    main = main.astype(BF)
    for part, coeff in enumerate((low, high)):

        @pl.loop(0, TAILW // STRIP)
        def _(step):
            near = pl.ds(pl.multiple_of(step * STRIP, STRIP), STRIP)
            cols = pl.ds(pl.multiple_of(part * TAILW + step * STRIP, STRIP), STRIP)
            found = matmul(main, head[:, :, cols].reshape(HEADS, STRIP))
            found = found + matmul(coeff, tail[:, :, near].reshape(TAILS, STRIP))
            if extra is not None:
                found = found + extra(cols)
            out[:, cols] = SCALE * found


def norm_backward(states, inverses, gain, upstream, out, gain_sum):
    @pl.loop(0, PAD // FOLD)
    def _(step):
        at = rows_of(step * FOLD)
        values, inverse, given = states[at, :].astype(F32), inverses[at, :], upstream[at, :]
        if out is not None:
            scaled = gain[...] * given
            inner = jnp.sum(scaled * values, axis=-1, keepdims=True)
            out[at, :] = scaled * inverse - values * inverse**3 * inner / WIDTH
        if gain_sum is not None:
            gain_sum[...] += given * values * inverse


def kernel(
    query, passage, gain, ask,
    query_grad, passage_grad, sums,
    query_embed, passage_embed, query_inv, passage_inv, swap,
    phead, ptail, qhead, qtail,
    asked, work, stage, landed, pool, pool_raw, pool_inv, pool_scores, pool_turned,
    terms, term_stage, term_landed,
    main_scores, rest_scores, total_out, totals, query_up, passage_up, gain_sum, held, run,
    ask_send, ask_recv, row_send, row_recv, term_send, term_recv,
    p_send, p_recv, q_send, q_recv, total_send, total_recv, sum_send, sum_recv,
):
    me, blk = lax.axis_index("group"), lax.axis_index("blk")
    z, plane = me // PLANE, me % PLANE
    barrier = pltpu.get_barrier_semaphore()

    @pl.loop(1, NGROUP)
    def _(turn):
        pl.semaphore_signal(barrier, inc=1, device_id={"group": peer(me, turn)}, device_id_type=MESH)

    for d in range(1, NBLK):
        pl.semaphore_signal(barrier, inc=1, device_id={"blk": (blk + d) % NBLK}, device_id_type=MESH)

    asked[0] = ask[...]
    embed(passage, gain, passage_embed, passage_inv)
    place_own(blk, passage_embed, phead, ptail)
    row, col = iota((FOLDW, FOLDW), 0), iota((FOLDW, FOLDW), 1)
    same = (row // FOLD == col % FOLD) & (row % FOLD == col // FOLD)
    swap[...] = jnp.where(same, 1.0, 0.0).astype(BF)
    pl.semaphore_wait(barrier, NGROUP - 1 + NBLK - 1)

    def asking(turn):
        return remote(
            ask, asked.at[turn], ask_send.at[turn], ask_recv.at[turn], group=peer(me, turn)
        )

    @pl.loop(1, NGROUP)
    def _(turn):
        asking(turn).start()

    ps = Spread(blk, phead, ptail, p_send, p_recv)
    qs = Spread(blk, qhead, qtail, q_send, q_recv)
    ps.hop(0, 1)
    embed(query, gain, query_embed, query_inv)
    place_own(blk, query_embed, qhead, qtail)

    @pl.loop(1, NGROUP)
    def _(turn):
        asking(turn).wait()

    lanes, turns = iota((NGROUP, 1, LANES), 2), iota((NGROUP, 1, LANES), 0)
    mine = (lanes // 128 == turns // 16) & ((lanes % 128) // SLOTS == turns % 16)
    wanted = jnp.sum(jnp.where(mine, asked[...], 0), axis=0)

    rows = Swap(me, stage, landed, row_send, row_recv, True)
    spread_steps = [
        lambda: ps.hop(4),
        lambda: ps.hop(2),
        lambda: ps.hop(3),
        lambda: ps.over(2, blk),
        lambda: ps.relay(0),
        lambda: ps.relay(1),
        lambda: ps.relay(4),
        lambda: ps.pass_near(),
    ]
    for step in range(CHUNKS):
        chunk = CHUNKS - 1 - step
        column = to_column(wanted[:, chunk * 128 : (chunk + 1) * 128], CROWS)
        pick = jnp.where(column - 1 == iota((CROWS, PAD), 1), 1.0, 0.0).astype(BF)
        fold_rows(pick, passage, None, swap, work, stage, None, chunk)
        for half in range(2):
            rows.start(chunk, half)
            spread_steps[2 * step + half]()
    landed[0:SLOTS] = stage[0:SLOTS]
    qs.hop(0, 1, 4)
    ps.pass_far()
    qs.hop(2, 3)
    qs.over(2, blk)
    ps.finish()

    main_hit, rest_hit, rest_valid = pair_masks(blk)
    main, rest = pair_scores(query_embed, phead, ptail)
    main_scores[...] = main
    rest_scores[...] = jnp.where(rest_valid, rest, -jnp.inf)

    for step in range(CHUNKS):
        chunk = CHUNKS - 1 - step
        rows.arrived(chunk)

        @pl.loop(0, CROWS // FOLD)
        def _(g):
            at = chunk * CROWS + g * FOLD
            tile = landed[pl.ds(at, FOLD)].reshape(FOLDW, FOLDW)
            flat = matmul(swap[...], tile)
            square = jnp.zeros((FOLD, FOLDW), F32)
            for k in range(FOLD):
                part = flat[k * FOLD : (k + 1) * FOLD]
                square = square + part * part
            inverse = lax.rsqrt(jnp.sum(square, axis=1, keepdims=True) / WIDTH + EPSILON)
            pool_inv[rows_of(at), :] = inverse
            for k in range(FOLD):
                part, cols = flat[k * FOLD : (k + 1) * FOLD], slice(k * FOLDW, (k + 1) * FOLDW)
                pool_raw[rows_of(at), cols] = part.astype(BF)
                pool[rows_of(at), cols] = (part * inverse * gain[:, cols]).astype(BF)

        here = pl.ds(chunk * CROWS, CROWS)
        pool_scores[chunk, :, 0:CROWS] = matmul_t(query_embed[...], pool[here, :]) * SCALE
        pool_turned[chunk, :, 0:PAD] = matmul_t(pool[here, :], query_embed[...]) * SCALE

    live = [ask[:, c * 128 : c * 128 + CROWS] > 0 for c in range(CHUNKS)]
    masked = [
        jnp.where(live[c], pool_scores[c, :, 0:CROWS], -jnp.inf) for c in range(CHUNKS)
    ]
    main, rest = main_scores[...], rest_scores[...]
    peak = jnp.maximum(
        jnp.max(main, axis=1, keepdims=True), jnp.max(rest, axis=1, keepdims=True)
    )
    for c in range(CHUNKS):
        peak = jnp.maximum(peak, jnp.max(masked[c], axis=1, keepdims=True))
    added = jnp.sum(jnp.exp(main - peak), axis=1, keepdims=True)
    added = added + jnp.sum(jnp.exp(rest - peak), axis=1, keepdims=True)
    for c in range(CHUNKS):
        added = added + jnp.sum(jnp.exp(masked[c] - peak), axis=1, keepdims=True)
    total = peak + jnp.log(added)
    square = iota((PAD, 128), 0) == iota((PAD, 128), 1)
    total_row = jnp.sum(jnp.where(square, total, 0.0), axis=0, keepdims=True)

    give = Swap(me, term_stage, term_landed, term_send, term_recv, False)
    q_steps = [
        lambda: qs.relay(0),
        lambda: qs.relay(1),
        lambda: qs.relay(4),
        lambda: qs.pass_near(),
    ]
    for step in range(CHUNKS):
        chunk = CHUNKS - 1 - step
        column = to_column(ask[:, chunk * 128 : (chunk + 1) * 128], CROWS)
        turned = jnp.exp(pool_turned[chunk, :, 0:PAD] - total_row[:, 0:PAD])
        turned = jnp.where(column > 0, turned, 0.0).astype(BF)
        fold_rows(turned, query_embed, SCALE, swap, work, term_stage, terms, chunk)
        give.start(chunk, 0)
        give.start(chunk, 1)
        if step == 0:
            total_out[...] = jnp.concatenate(
                [
                    jnp.sum(jnp.where(main_hit, total, 0.0), axis=0, keepdims=True),
                    jnp.sum(jnp.where(rest_hit, total, 0.0), axis=0, keepdims=True),
                ],
                axis=1,
            )
            totals[blk] = total_out[...]
            total_copies = [
                remote(
                    total_out, totals.at[blk], total_send.at[d], total_recv.at[d],
                    blk=(blk + d) % NBLK,
                )
                for d in range(1, NBLK)
            ]
            for copy in total_copies:
                copy.start()
        q_steps[step]()
    term_landed[0:SLOTS] = term_stage[0:SLOTS]

    gain_sum[...] = jnp.zeros_like(gain_sum)
    main = jnp.exp(main - total) - jnp.where(main_hit, 1.0, 0.0)
    rest = jnp.where(rest_valid, jnp.exp(rest - total), 0.0) - jnp.where(rest_hit, 1.0, 0.0)
    coeffs = [jnp.exp(masked[c] - total).astype(BF) for c in range(CHUNKS)]

    def from_pool(cols):
        found = matmul(coeffs[0], pool[0:CROWS, cols])
        for c in range(1, CHUNKS):
            found = found + matmul(coeffs[c], pool[c * CROWS : (c + 1) * CROWS, cols])
        return found

    pair_grads(main, rest, phead, ptail, query_up, from_pool)
    norm_backward(query, query_inv, gain, query_up, query_grad, gain_sum)

    @pl.loop(0, POOL // FOLD)
    def _(g):
        at = rows_of(g * FOLD)
        gain_sum[...] += terms[at, :].astype(F32) * (pool_raw[at, :].astype(F32) * pool_inv[at, :])

    positive = jnp.sum(jnp.where(main_hit, main_scores[...], 0.0), axis=1, keepdims=True)
    positive = positive + jnp.sum(jnp.where(rest_hit, rest_scores[...], 0.0), axis=1, keepdims=True)
    loss = jnp.where(iota((PAD, 128), 0) < ROWS, total - positive, 0.0)
    loss = jnp.sum(loss, axis=0, keepdims=True)

    qs.pass_far()
    qs.finish()
    for copy in total_copies:
        copy.wait()
    lane_totals = totals[0]
    for b in range(1, NBLK):
        lane_totals = lane_totals + totals[b]
    main, rest = pair_scores(passage_embed, qhead, qtail)
    main = jnp.exp(main - lane_totals[:, :HEADS]) - jnp.where(main_hit, 1.0, 0.0)
    rest = jnp.exp(rest - lane_totals[:, HEADS:]) - jnp.where(rest_hit, 1.0, 0.0)
    rest = jnp.where(rest_valid, rest, 0.0)
    pair_grads(main, rest, qhead, qtail, passage_up, None)
    norm_backward(passage, passage_inv, gain, passage_up, None, gain_sum)

    run[0, :, 0:WIDTH] = jnp.sum(gain_sum[...], axis=0, keepdims=True)
    run[0, :, WIDTH:GAINS] = loss
    where = [
        lambda d: {"blk": (blk + d) % NBLK},
        lambda d: {"group": ((z + d) % NZ) * PLANE + plane},
        lambda d: {"group": z * PLANE + (plane + d) % PLANE},
    ]
    slots = (blk, z, plane)

    def sum_copies(level):
        return [
            remote(
                run.at[level], held.at[level, slots[level]],
                sum_send.at[level, d], sum_recv.at[level, d], **where[level](d),
            )
            for d in range(1, 8)
        ]

    def sum_start(level):
        held[level, slots[level]] = run[level]
        for copy in sum_copies(level):
            copy.start()

    def sum_end(level):
        for copy in sum_copies(level):
            copy.wait()
        got = held[level, 0]
        for d in range(1, 8):
            got = got + held[level, d]
        if level < 2:
            run[level + 1] = got
        else:
            sums[...] = got

    sum_start(0)
    for step in range(CHUNKS):
        chunk = CHUNKS - 1 - step
        give.arrived(chunk)

        @pl.loop(0, CROWS // FOLD)
        def _(g):
            at = chunk * CROWS + g * FOLD
            tile = term_landed[pl.ds(at, FOLD)].reshape(FOLDW, FOLDW)
            flat = matmul(swap[...], tile).astype(BF)
            for k in range(FOLD):
                terms[rows_of(at), k * FOLDW : (k + 1) * FOLDW] = flat[k * FOLD : (k + 1) * FOLD]

        if step == 1:
            sum_end(0)
            sum_start(1)
        if step == 3:
            sum_end(1)
            sum_start(2)

    names = [
        jnp.where(iota((PAD, CROWS), 0) + 1 == wanted[:, c * 128 : c * 128 + CROWS], 1.0, 0.0).astype(BF)
        for c in range(CHUNKS)
    ]

    @pl.loop(0, WIDTH // STRIP)
    def _(step):
        cols = pl.ds(pl.multiple_of(step * STRIP, STRIP), STRIP)
        found = passage_up[:, cols]
        for c in range(CHUNKS):
            found = found + matmul(names[c], terms[c * CROWS : (c + 1) * CROWS, cols])
        passage_up[:, cols] = found

    norm_backward(passage, passage_inv, gain, passage_up, passage_grad, None)
    sum_end(2)
    ps.sent()
    qs.sent()
    rows.sent()
    give.sent()


def requests(me, negative_owner, negative_row):
    entries = negative_owner.size
    turn = turn_of(me, negative_owner.reshape(entries))
    at = jnp.arange(entries, dtype=I32)
    rank = jnp.sum(
        jnp.where((turn[:, None] == turn[None, :]) & (at[None, :] < at[:, None]), 1, 0), axis=1
    )
    lane = (turn // 16) * 128 + (turn % 16) * SLOTS + rank
    hit = lane[:, None] == jnp.arange(LANES, dtype=I32)[None, :]
    return jnp.sum(jnp.where(hit, negative_row.reshape(entries)[:, None] + 1, 0), axis=0)[None, :]


def local(query_states, passage_states, norm_gain, negative_owner, negative_row):
    ask = requests(lax.axis_index("group"), negative_owner, negative_row)
    more = ((0, PAD - ROWS), (0, 0))
    vmem = pl.BlockSpec(memory_space=pltpu.VMEM)
    dma = pltpu.SemaphoreType.DMA
    query_grad, passage_grad, sums = pl.pallas_call(
        kernel,
        out_shape=(
            jax.ShapeDtypeStruct((PAD, WIDTH), F32),
            jax.ShapeDtypeStruct((PAD, WIDTH), F32),
            jax.ShapeDtypeStruct((1, GAINS), F32),
        ),
        in_specs=[vmem] * 4,
        out_specs=(vmem,) * 3,
        scratch_shapes=[
            pltpu.VMEM((PAD, WIDTH), BF),
            pltpu.VMEM((PAD, WIDTH), BF),
            pltpu.VMEM((PAD, 1), F32),
            pltpu.VMEM((PAD, 1), F32),
            pltpu.VMEM((FOLDW, FOLDW), BF),
            pltpu.VMEM((NBLK, HEAD, WIDTH), BF),
            pltpu.VMEM((NBLK, FOLD, TAILW), BF),
            pltpu.VMEM((NBLK, HEAD, WIDTH), BF),
            pltpu.VMEM((NBLK, FOLD, TAILW), BF),
            pltpu.VMEM((NGROUP, 1, LANES), I32),
            pltpu.VMEM((CROWS // FOLD, FOLDW, FOLDW), BF),
            pltpu.VMEM((POOL, FOLD, FOLDW), BF),
            pltpu.VMEM((POOL, FOLD, FOLDW), BF),
            pltpu.VMEM((POOL, WIDTH), BF),
            pltpu.VMEM((POOL, WIDTH), BF),
            pltpu.VMEM((POOL, 1), F32),
            pltpu.VMEM((CHUNKS, PAD, 128), F32),
            pltpu.VMEM((CHUNKS, CROWS, 128), F32),
            pltpu.VMEM((POOL, WIDTH), BF),
            pltpu.VMEM((POOL, FOLD, FOLDW), BF),
            pltpu.VMEM((POOL, FOLD, FOLDW), BF),
            pltpu.VMEM((PAD, HEADS), F32),
            pltpu.VMEM((PAD, TAILS), F32),
            pltpu.VMEM((1, HEADS + TAILS), F32),
            pltpu.VMEM((NBLK, 1, HEADS + TAILS), F32),
            pltpu.VMEM((PAD, WIDTH), F32),
            pltpu.VMEM((PAD, WIDTH), F32),
            pltpu.VMEM((FOLD, WIDTH), F32),
            pltpu.VMEM((3, 8, 1, GAINS), F32),
            pltpu.VMEM((3, 1, GAINS), F32),
            *[dma((NGROUP,))] * 6,
            *[dma((8, 5))] * 4,
            *[dma((NBLK,))] * 2,
            *[dma((3, 8))] * 2,
        ],
        compiler_params=pltpu.CompilerParams(
            collective_id=0, has_side_effects=True, vmem_limit_bytes=VMEM_LIMIT
        ),
    )(jnp.pad(query_states, more), jnp.pad(passage_states, more), norm_gain[None, :], ask)
    loss = sums[0, WIDTH] / (ROWS * NBLK * NGROUP)
    return (query_grad[:ROWS], passage_grad[:ROWS], sums[0, :WIDTH], loss)

def solution(mesh):
    return jax.shard_map(
        local,
        mesh=mesh,
        in_specs=(
            P(("blk", "group"), None),
            P(("blk", "group"), None),
            P(),
            P(("blk", "group"), None),
            P(("blk", "group"), None),
        ),
        out_specs=(P(("blk", "group"), None), P(("blk", "group"), None), P(), P()),
        check_vma=False,
    )
```

time: 410 us -> 213 us (0.52)
  Pallas kernels: 0 us -> 199 us
  blocking collectives: 187 us -> 0 us
  waiting for transfers between devices: 115 us -> 0 us
  matrix products: 25.3 us -> 0 us
  local copies, waits for them, and re-layouts: 28.1 us -> 9.28 us
  starting transfers between devices: 18.2 us -> 0 us
  other arithmetic: 18.2 us -> 1.77 us
  between operations: 17 us -> 2.51 us
    pallas_call x0 -> x1, Pallas kernels: none -> 199 us  [local(): pl.pallas_call(kernel, out_shape=(jax.ShapeDtypeStruct((PAD, WIDTH), F32)...]
    all_to_all x2 -> x0, waiting for transfers between devices: 115 us -> none  [the longest x1 105 us: local(): lax.all_to_all(found_rows, 'group', split_axis=0, concat_axis=0, tiled=True)]
    psum x1 -> x0, blocking collectives: 100 us -> none  [local(): lax.psum((gain_query + gain_passage, loss_part), ('blk', 'group'))]
    unnamed x1 -> x0, blocking collectives: 62.5 us -> none
    dot_general x7 -> x0, matrix products: 25.3 us -> none  [the longest x1 7.65 us: local(): jnp.einsum('qp,qd->pd', coefficient, all_queries, preferred_element_type=...]
    all_to_all x1 -> x0, blocking collectives: 24.4 us -> none  [local(): lax.all_to_all(request, 'group', split_axis=0, concat_axis=0, tiled=True)]
    all_to_all x2 -> x0, starting transfers between devices: 18.2 us -> none  [the longest x1 12.5 us: local(): lax.all_to_all(pool_terms.reshape(groups, capacity, width), 'group', spli...]
    reshape x4 -> x1, local copies, waits for them, and re-layouts: 11.7 us -> 0.1 us  [requests(): turn = turn_of(me, negative_owner.reshape(entries))]
  transfers between devices with their start and end apart: 4 -> 0, of which waited for: 2 -> 0; matrix products, arithmetic and copies ran while one was open for 14% -> 0% of each run, Pallas kernels for 0% -> 0%
where the time goes in v1:
time: 213 us; the launch traced here: 212 us
  Pallas kernels  199 us (93%)
  local copies, waits for them, and re-layouts  9.28 us (4%)
  between operations  2.51 us (1%)
    pallas_call x1, Pallas kernels, local(): pl.pallas_call(kernel, out_shape=(jax.ShapeDtypeStruct((PAD, WIDTH), F32)...  199 us

profile of v1, /device:TPU:1, one launch (start us, length us, event | category | flops | bytes accessed | tf_op | source)
XLA Modules:
  0.0 212.2 jit_solution(4107771025331947534)
XLA Ops:
  0.6 0.0 copy-start.1
  0.7 0.7 broadcast_add_fusion
  1.4 0.1 copy.12
  1.5 0.1 add.210
  1.6 0.8 copy.11
  2.4 0.1 reshape.299
  2.5 0.2 select_reduce_fusion.1
  2.8 0.7 select_reduce_fusion
  3.5 2.0 pad.7.query
  5.5 0.0 copy-done.1
  5.5 0.9 pad.8.passage
  6.4 198.6 %shard_map.84 = (f32[80,4096]{1,0:T(8,128)}, f32[80,4096]{1,0:T(8,128)}, f32[1,4224]{1,0:T(1,128)}) custom-call(bf16[80,4096]{1,0:T(8,128)(2,1)} %pad.7.query, bf16[80,4096]{1,0:T(8,128)(2,1)} %pad.8.passage, f32[1,4096]{1,0:T(1,128)} %bitcast.5, s32[1,512]{1,0:T(1,128)} %bitcast.6), custom_call_target="tpu_custom_call" | custom-call | tf_op jit(solution)/shard_map/pallas_call | solution.py:565
  205.0 0.0 copy-start.2
  205.0 0.0 copy-start
  205.0 1.3 slice.15
  207.0 2.4 %slice.12 = f32[72,4096]{1,0:T(8,128)} slice(f32[80,4096]{1,0:T(8,128)} %get-tuple-element.7), slice={[0:72], [0:4096]} | slice | bytes 2359296 | tf_op jit(solution)/shard_map/slice | solution.py:615
  209.3 0.0 copy-done.2
  209.3 0.6 slice.14
  209.9 0.0 copy-done
  209.9 1.1 slice.13
  (2 shorter events, 0.1 us)
Async XLA Ops:
  0.6 4.9 %copy-start.1 = (bf16[72,4096]{1,0:T(8,128)(2,1)S(1)}, bf16[72,4096]{1,0:T(8,128)(2,1)}, u32[]{:S(2)}) copy-start(bf16[72,4096]{1,0:T(8,128)(2,1)} %param.6) | copy-start | bytes 1769476
  205.0 4.3 %copy-start.2 = (f32[1,4224]{1,0:T(1,128)S(1)}, f32[1,4224]{1,0:T(1,128)}, u32[]{:S(2)}) copy-start(f32[1,4224]{1,0:T(1,128)} %get-tuple-element.9) | copy-start | bytes 50692
  205.0 4.9 %copy-start = (f32[80,4096]{1,0:T(8,128)S(1)}, f32[80,4096]{1,0:T(8,128)}, u32[]{:S(2)}) copy-start(f32[80,4096]{1,0:T(8,128)} %get-tuple-element.8) | copy-start | bytes 3932164

commit v2 on v1

--- a/solution.py
+++ b/solution.py
@@ -25,31 +25,51 @@
 HEAD, TAILW = 64, 2048
 HEADS, TAILS = NBLK * HEAD, NBLK * FOLD
 STRIP = 512
+DZ = (0, 1, 7, 4, 2, 6, 3, 5)
+ORDER = (1, 0, 3, 2)
 SCALE = 4.0 / math.sqrt(WIDTH)
 GAINS = WIDTH + 128
 VMEM_LIMIT = 60 * 1024 * 1024
 BF, F32, I32 = jnp.bfloat16, jnp.float32, jnp.int32
 
 
-def turn_z(place):
-    odd, half = place % 2, place // 2
-    return (1 - odd) * half + odd * (NZ - 1 - half)
-
-
-def peer(me, turn, back=False):
-    z, y, x = me // (NY * NX), (me // NX) % NY, me % NX
-    dz, dy, dx = turn_z(turn // (NY * NX)), (turn // NX) % NY, turn % NX
-    if back:
-        dz, dx = NZ - dz, NX - dx
-    return (((z + dz) % NZ) * NY + (y + dy) % NY) * NX + (x + dx) % NX
+class Peers:
+    def __init__(self, me, back=False):
+        self.z, self.y, self.x = me // PLANE, (me // NX) % NY, me % NX
+        self.back = back
+
+    def plane(self, dy, dx):
+        x = self.x + NX - dx if self.back else self.x + dx
+        return ((self.y + dy) % NY) * NX + x % NX
+
+    def level(self, place):
+        dz = DZ[place]
+        return (self.z + NZ - dz if self.back else self.z + dz) % NZ
+
+    def all(self, act):
+        levels = [self.level(place) for place in range(NZ)]
+
+        @pl.loop(0, NX)
+        def _(dx):
+            for dy in range(NY):
+                plane = self.plane(dy, dx)
+                for place in range(NZ):
+                    turn, other = (dy * NZ + place) * NX + dx, levels[place] * PLANE + plane
+                    if dy > 0 or place > 0:
+                        act(turn, other)
+                    else:
+
+                        @pl.when(dx > 0)
+                        def _():
+                            act(turn, other)
 
 
 def turn_of(me, other):
     dz = (other // (NY * NX) - me // (NY * NX)) % NZ
     dy = ((other // NX) % NY - (me // NX) % NY) % NY
     dx = (other % NX - me % NX) % NX
-    place = jnp.where(dz < NZ // 2, 2 * dz, 2 * (NZ - 1 - dz) + 1)
-    return (place * NY + dy) * NX + dx
+    place = sum(jnp.where(dz == step, at, 0) for at, step in enumerate(DZ))
+    return (dy * NZ + place) * NX + dx
 
 
 def remote(src, dst, send, recv, **where):
@@ -132,38 +152,41 @@
 
 
 class Swap:
-    def __init__(self, me, src, dst, send, recv, back):
-        self.me, self.src, self.dst, self.send, self.recv, self.back = me, src, dst, send, recv, back
-
-    def each(self, chunk, first, count, act):
-        @pl.loop(first, first + count)
-        def _(plane):
-            for side in range(2):
-                turn = (2 * chunk + side) * PLANE + plane
-
-                @pl.when(turn > 0)
-                def _():
-                    rows = pl.ds(turn * SLOTS, SLOTS)
-                    act(
-                        remote(
-                            self.src.at[rows],
-                            self.dst.at[rows],
-                            self.send.at[turn],
-                            self.recv.at[turn],
-                            group=peer(self.me, turn, self.back),
-                        )
-                    )
+    def __init__(self, peers, src, dst, send, recv):
+        self.peers, self.src, self.dst, self.send, self.recv = peers, src, dst, send, recv
+
+    def message(self, turn, other):
+        rows = pl.ds(turn * SLOTS, SLOTS)
+        return remote(
+            self.src.at[rows], self.dst.at[rows], self.send.at[turn], self.recv.at[turn], group=other
+        )
 
     def start(self, chunk, half):
-        self.each(chunk, half * (PLANE // 2), PLANE // 2, lambda copy: copy.start())
+        dy = chunk // 2
+
+        @pl.loop(half * (NX // 2), (half + 1) * (NX // 2))
+        def _(dx):
+            plane = self.peers.plane(dy, dx)
+            for place in range((chunk % 2) * (NZ // 2), (chunk % 2 + 1) * (NZ // 2)):
+                turn = (dy * NZ + place) * NX + dx
+                copy = self.message(turn, self.peers.level(place) * PLANE + plane)
+                if dy > 0 or place > 0:
+                    copy.start()
+                else:
+
+                    @pl.when(dx > 0)
+                    def _():
+                        copy.start()
 
     def arrived(self, chunk):
-        self.each(chunk, 0, PLANE, lambda copy: copy.wait_recv())
+        @pl.loop(max(1, 2 * PLANE * chunk), 2 * PLANE * (chunk + 1))
+        def _(turn):
+            self.message(turn, 0).wait_recv()
 
     def sent(self):
-        @pl.loop(0, CHUNKS)
-        def _(chunk):
-            self.each(chunk, 0, PLANE, lambda copy: copy.wait_send())
+        @pl.loop(1, NGROUP)
+        def _(turn):
+            self.message(turn, 0).wait_send()
 
 
 def iota(shape, dim):
@@ -258,24 +281,45 @@
 
 
 def norm_backward(states, inverses, gain, upstream, out, gain_sum):
-    @pl.loop(0, PAD // FOLD)
-    def _(step):
-        at = rows_of(step * FOLD)
+    def rows(at, count):
         values, inverse, given = states[at, :].astype(F32), inverses[at, :], upstream[at, :]
         if out is not None:
             scaled = gain[...] * given
             inner = jnp.sum(scaled * values, axis=-1, keepdims=True)
-            out[at, :] = scaled * inverse - values * inverse**3 * inner / WIDTH
+            found = scaled * inverse - values * inverse**3 * inner / WIDTH
+            out[pl.ds(at.start, count), :] = found[:count]
         if gain_sum is not None:
             gain_sum[...] += given * values * inverse
 
+    @pl.loop(0, HEAD // FOLD)
+    def _(step):
+        rows(rows_of(step * FOLD), FOLD)
+
+    rows(pl.ds(HEAD, FOLD), ROWS - HEAD)
+
+
+def requests(me, owner, row, ask):
+    turns = [turn_of(me, owner[:, k : k + 1]) for k in range(owner.shape[1])]
+    down, across = iota((ROWS, 128), 0), iota((ROWS, 128), 1)
+    lines = [jnp.sum(jnp.where(down == across, turn, 0), axis=0, keepdims=True) for turn in turns]
+    found = jnp.zeros((1, LANES), I32)
+    for k, turn in enumerate(turns):
+        earlier = jnp.where((turn == lines[k]) & (across < down), 1, 0)
+        for line in lines[:k]:
+            earlier = earlier + jnp.where((turn == line) & (across < ROWS), 1, 0)
+        rank = jnp.sum(earlier, axis=1, keepdims=True)
+        lane = (turn // 16) * 128 + (turn % 16) * SLOTS + rank
+        hit = lane == iota((ROWS, LANES), 1)
+        found = found + jnp.sum(jnp.where(hit, row[:, k : k + 1] + 1, 0), axis=0, keepdims=True)
+    ask[...] = found
+
 
 def kernel(
-    query, passage, gain, ask,
+    both, gain, owner, row_asked,
     query_grad, passage_grad, sums,
-    query_embed, passage_embed, query_inv, passage_inv, swap,
+    query, passage, ask, query_embed, passage_embed, query_inv, passage_inv, swap,
     phead, ptail, qhead, qtail,
-    asked, work, stage, landed, pool, pool_raw, pool_inv, pool_scores, pool_turned,
+    asked, mine, work, stage, landed, pool, pool_raw, pool_inv, pool_scores, pool_turned,
     terms, term_stage, term_landed,
     main_scores, rest_scores, total_out, totals, query_up, passage_up, gain_sum, held, run,
     ask_send, ask_recv, row_send, row_recv, term_send, term_recv,
@@ -285,29 +329,38 @@
     z, plane = me // PLANE, me % PLANE
     barrier = pltpu.get_barrier_semaphore()
 
-    @pl.loop(1, NGROUP)
-    def _(turn):
-        pl.semaphore_signal(barrier, inc=1, device_id={"group": peer(me, turn)}, device_id_type=MESH)
+    there, back = Peers(me), Peers(me, True)
+
+    there.all(
+        lambda turn, other: pl.semaphore_signal(
+            barrier, inc=1, device_id={"group": other}, device_id_type=MESH
+        )
+    )
 
     for d in range(1, NBLK):
         pl.semaphore_signal(barrier, inc=1, device_id={"blk": (blk + d) % NBLK}, device_id_type=MESH)
 
+    requests(me, owner, row_asked, ask)
     asked[0] = ask[...]
+    query[0:HEAD] = both[0:HEAD]
+    passage[0:HEAD] = both[HEAD : 2 * HEAD]
+    last, none = both[2 * HEAD : 2 * ROWS].astype(F32), jnp.zeros((PAD - ROWS, WIDTH), F32)
+    query[HEAD:PAD] = jnp.concatenate([last[: ROWS - HEAD], none], axis=0).astype(BF)
+    passage[HEAD:PAD] = jnp.concatenate([last[ROWS - HEAD :], none], axis=0).astype(BF)
     embed(passage, gain, passage_embed, passage_inv)
     place_own(blk, passage_embed, phead, ptail)
     row, col = iota((FOLDW, FOLDW), 0), iota((FOLDW, FOLDW), 1)
     same = (row // FOLD == col % FOLD) & (row % FOLD == col // FOLD)
     swap[...] = jnp.where(same, 1.0, 0.0).astype(BF)
+    turns = iota((NGROUP, 1, LANES), 0)
+    past = iota((NGROUP, 1, LANES), 2) - (turns // 16) * 128 - (turns % 16) * SLOTS
+    mine[...] = jnp.where((past >= 0) & (past < SLOTS), 1, 0)
     pl.semaphore_wait(barrier, NGROUP - 1 + NBLK - 1)
 
-    def asking(turn):
-        return remote(
-            ask, asked.at[turn], ask_send.at[turn], ask_recv.at[turn], group=peer(me, turn)
-        )
-
-    @pl.loop(1, NGROUP)
-    def _(turn):
-        asking(turn).start()
+    def asking(turn, other):
+        return remote(ask, asked.at[turn], ask_send.at[turn], ask_recv.at[turn], group=other)
+
+    there.all(lambda turn, other: asking(turn, other).start())
 
     ps = Spread(blk, phead, ptail, p_send, p_recv)
     qs = Spread(blk, qhead, qtail, q_send, q_recv)
@@ -317,25 +370,23 @@
 
     @pl.loop(1, NGROUP)
     def _(turn):
-        asking(turn).wait()
-
-    lanes, turns = iota((NGROUP, 1, LANES), 2), iota((NGROUP, 1, LANES), 0)
-    mine = (lanes // 128 == turns // 16) & ((lanes % 128) // SLOTS == turns % 16)
-    wanted = jnp.sum(jnp.where(mine, asked[...], 0), axis=0)
-
-    rows = Swap(me, stage, landed, row_send, row_recv, True)
+        asking(turn, 0).wait()
+
+    wanted = jnp.sum(asked[...] * mine[...], axis=0)
+
+    rows = Swap(back, stage, landed, row_send, row_recv)
     spread_steps = [
         lambda: ps.hop(4),
         lambda: ps.hop(2),
         lambda: ps.hop(3),
-        lambda: ps.over(2, blk),
-        lambda: ps.relay(0),
+        lambda: (ps.over(2, blk), ps.relay(0)),
         lambda: ps.relay(1),
         lambda: ps.relay(4),
         lambda: ps.pass_near(),
+        lambda: None,
     ]
     for step in range(CHUNKS):
-        chunk = CHUNKS - 1 - step
+        chunk = ORDER[step]
         column = to_column(wanted[:, chunk * 128 : (chunk + 1) * 128], CROWS)
         pick = jnp.where(column - 1 == iota((CROWS, PAD), 1), 1.0, 0.0).astype(BF)
         fold_rows(pick, passage, None, swap, work, stage, None, chunk)
@@ -345,8 +396,6 @@
     landed[0:SLOTS] = stage[0:SLOTS]
     qs.hop(0, 1, 4)
     ps.pass_far()
-    qs.hop(2, 3)
-    qs.over(2, blk)
     ps.finish()
 
     main_hit, rest_hit, rest_valid = pair_masks(blk)
@@ -355,7 +404,7 @@
     rest_scores[...] = jnp.where(rest_valid, rest, -jnp.inf)
 
     for step in range(CHUNKS):
-        chunk = CHUNKS - 1 - step
+        chunk = ORDER[step]
         rows.arrived(chunk)
 
         @pl.loop(0, CROWS // FOLD)
@@ -396,20 +445,25 @@
     square = iota((PAD, 128), 0) == iota((PAD, 128), 1)
     total_row = jnp.sum(jnp.where(square, total, 0.0), axis=0, keepdims=True)
 
-    give = Swap(me, term_stage, term_landed, term_send, term_recv, False)
+    give = Swap(there, term_stage, term_landed, term_send, term_recv)
     q_steps = [
         lambda: qs.relay(0),
-        lambda: qs.relay(1),
         lambda: qs.relay(4),
         lambda: qs.pass_near(),
+        lambda: qs.pass_far(),
     ]
     for step in range(CHUNKS):
-        chunk = CHUNKS - 1 - step
+        chunk = ORDER[step]
         column = to_column(ask[:, chunk * 128 : (chunk + 1) * 128], CROWS)
         turned = jnp.exp(pool_turned[chunk, :, 0:PAD] - total_row[:, 0:PAD])
         turned = jnp.where(column > 0, turned, 0.0).astype(BF)
         fold_rows(turned, query_embed, SCALE, swap, work, term_stage, terms, chunk)
         give.start(chunk, 0)
+        if step == 0:
+            qs.hop(2, 3)
+            qs.over(2, blk)
+        if step == 1:
+            qs.relay(1)
         give.start(chunk, 1)
         if step == 0:
             total_out[...] = jnp.concatenate(
@@ -456,7 +510,6 @@
     loss = jnp.where(iota((PAD, 128), 0) < ROWS, total - positive, 0.0)
     loss = jnp.sum(loss, axis=0, keepdims=True)
 
-    qs.pass_far()
     qs.finish()
     for copy in total_copies:
         copy.wait()
@@ -506,8 +559,10 @@
 
     sum_start(0)
     for step in range(CHUNKS):
-        chunk = CHUNKS - 1 - step
+        chunk = ORDER[step]
         give.arrived(chunk)
+        lanes = slice(chunk * 128, chunk * 128 + CROWS)
+        names = jnp.where(iota((PAD, CROWS), 0) + 1 == wanted[:, lanes], 1.0, 0.0).astype(BF)
 
         @pl.loop(0, CROWS // FOLD)
         def _(g):
@@ -520,7 +575,7 @@
         if step == 1:
             sum_end(0)
             sum_start(1)
-        if step == 3:
+        if step == 2:
             sum_end(1)
             sum_start(2)
 
@@ -545,33 +600,28 @@
     give.sent()
 
 
-def requests(me, negative_owner, negative_row):
-    entries = negative_owner.size
-    turn = turn_of(me, negative_owner.reshape(entries))
-    at = jnp.arange(entries, dtype=I32)
-    rank = jnp.sum(
-        jnp.where((turn[:, None] == turn[None, :]) & (at[None, :] < at[:, None]), 1, 0), axis=1
+def local(query_states, passage_states, norm_gain, negative_owner, negative_row):
+    both = jnp.concatenate(
+        [
+            query_states[:HEAD], passage_states[:HEAD],
+            query_states[HEAD:], passage_states[HEAD:],
+        ]
     )
-    lane = (turn // 16) * 128 + (turn % 16) * SLOTS + rank
-    hit = lane[:, None] == jnp.arange(LANES, dtype=I32)[None, :]
-    return jnp.sum(jnp.where(hit, negative_row.reshape(entries)[:, None] + 1, 0), axis=0)[None, :]
-
-
-def local(query_states, passage_states, norm_gain, negative_owner, negative_row):
-    ask = requests(lax.axis_index("group"), negative_owner, negative_row)
-    more = ((0, PAD - ROWS), (0, 0))
     vmem = pl.BlockSpec(memory_space=pltpu.VMEM)
     dma = pltpu.SemaphoreType.DMA
     query_grad, passage_grad, sums = pl.pallas_call(
         kernel,
         out_shape=(
-            jax.ShapeDtypeStruct((PAD, WIDTH), F32),
-            jax.ShapeDtypeStruct((PAD, WIDTH), F32),
+            jax.ShapeDtypeStruct((ROWS, WIDTH), F32),
+            jax.ShapeDtypeStruct((ROWS, WIDTH), F32),
             jax.ShapeDtypeStruct((1, GAINS), F32),
         ),
         in_specs=[vmem] * 4,
         out_specs=(vmem,) * 3,
         scratch_shapes=[
+            pltpu.VMEM((PAD, WIDTH), BF),
+            pltpu.VMEM((PAD, WIDTH), BF),
+            pltpu.VMEM((1, LANES), I32),
             pltpu.VMEM((PAD, WIDTH), BF),
             pltpu.VMEM((PAD, WIDTH), BF),
             pltpu.VMEM((PAD, 1), F32),
@@ -581,6 +631,7 @@
             pltpu.VMEM((NBLK, FOLD, TAILW), BF),
             pltpu.VMEM((NBLK, HEAD, WIDTH), BF),
             pltpu.VMEM((NBLK, FOLD, TAILW), BF),
+            pltpu.VMEM((NGROUP, 1, LANES), I32),
             pltpu.VMEM((NGROUP, 1, LANES), I32),
             pltpu.VMEM((CROWS // FOLD, FOLDW, FOLDW), BF),
             pltpu.VMEM((POOL, FOLD, FOLDW), BF),
@@ -610,9 +661,9 @@
         compiler_params=pltpu.CompilerParams(
             collective_id=0, has_side_effects=True, vmem_limit_bytes=VMEM_LIMIT
         ),
-    )(jnp.pad(query_states, more), jnp.pad(passage_states, more), norm_gain[None, :], ask)
+    )(both, norm_gain[None, :], negative_owner, negative_row)
     loss = sums[0, WIDTH] / (ROWS * NBLK * NGROUP)
-    return (query_grad[:ROWS], passage_grad[:ROWS], sums[0, :WIDTH], loss)
+    return (query_grad, passage_grad, sums[0, :WIDTH], loss)
 
 def solution(mesh):
     return jax.shard_map(

time: 213 us -> 195 us (0.915)
  Pallas kernels: 199 us -> 181 us
    pallas_call x1, Pallas kernels: 199 us -> 181 us  [local(): pl.pallas_call(kernel, out_shape=(jax.ShapeDtypeStruct((ROWS, WIDTH), F32...]
    unnamed x7 -> x6, local copies, waits for them, and re-layouts: 0.79 us -> 6.24 us
    pad x2 -> x0, local copies, waits for them, and re-layouts: 2.84 us -> none  [the longest x1 1.95 us: local(): jnp.pad(query_states, more)]
where the time goes in v2:
time: 195 us; the launch traced here: 194 us
  Pallas kernels  181 us (93%)
  local copies, waits for them, and re-layouts  9.92 us (5%)
  between operations  2.43 us (1%)
    pallas_call x1, Pallas kernels, local(): pl.pallas_call(kernel, out_shape=(jax.ShapeDtypeStruct((ROWS, WIDTH), F32...  181 us
    unnamed x6, local copies, waits for them, and re-layouts  6.24 us

profile of v2, /device:TPU:1, one launch (start us, length us, event | category | flops | bytes accessed | tf_op | source)
XLA Modules:
  0.0 194.4 jit_solution(14244533200001580352)
XLA Ops:
  0.6 1.4 copy.9.owner
  2.0 1.4 copy.10.row_asked
  3.4 0.0 slice-start
  3.4 0.0 slice-start.1
  3.4 0.0 slice-start.2
  3.4 0.0 slice-start.3
  3.4 0.8 slice-done
  4.2 0.2 slice-done.1
  4.5 0.0 slice-done.2
  4.5 0.2 slice-done.3
  4.7 1.1 pad_maximum_fusion.both
  5.7 181.0 %shard_map.84 = (f32[72,4096]{1,0:T(8,128)}, f32[72,4096]{1,0:T(8,128)}, f32[1,4224]{1,0:T(1,128)}) custom-call(bf16[144,4096]{1,0:T(8,128)(2,1)} %pad_maximum_fusion.both, f32[1,4096]{1,0:T(1,128)} %bitcast.3, s32[72,4]{1,0:T(8,128)} %copy.9.owner, s32[72,4]{1,0:T(8,128)} %copy.10.row_asked), custom_call_target="tpu_custom_call" | custom-call | tf_op jit(solution)/shard_map/pallas_call | solution.py:612
  186.7 1.1 slice.23
  188.5 1.3 slice.22
  189.8 0.0 copy-start
  189.8 2.5 %copy.13 = f32[72,4096]{1,0:T(8,128)} copy(f32[72,4096]{1,0:T(8,128)} %get-tuple-element.14) | data formatting | bytes 2359296
  192.3 0.0 copy-done
  192.3 1.0 copy.14
Async XLA Ops:
  3.4 0.8 slice-start
  3.4 1.1 slice-start.1
  3.4 1.1 slice-start.2
  3.4 1.3 slice-start.3
  189.8 2.5 %copy-start = (f32[72,4096]{1,0:T(8,128)S(1)}, f32[72,4096]{1,0:T(8,128)}, u32[]{:S(2)}) copy-start(f32[72,4096]{1,0:T(8,128)} %get-tuple-element.15) | copy-start | bytes 3538948

commit v3 on v2

--- a/solution.py
+++ b/solution.py
@@ -395,16 +395,17 @@
             spread_steps[2 * step + half]()
     landed[0:SLOTS] = stage[0:SLOTS]
     qs.hop(0, 1, 4)
-    ps.pass_far()
-    ps.finish()
-
     main_hit, rest_hit, rest_valid = pair_masks(blk)
-    main, rest = pair_scores(query_embed, phead, ptail)
-    main_scores[...] = main
-    rest_scores[...] = jnp.where(rest_valid, rest, -jnp.inf)
 
     for step in range(CHUNKS):
         chunk = ORDER[step]
+        if step == 1:
+            ps.pass_far()
+        if step == 2:
+            ps.finish()
+            main, rest = pair_scores(query_embed, phead, ptail)
+            main_scores[...] = main
+            rest_scores[...] = jnp.where(rest_valid, rest, -jnp.inf)
         rows.arrived(chunk)
 
         @pl.loop(0, CROWS // FOLD)
@@ -510,6 +511,20 @@
     loss = jnp.where(iota((PAD, 128), 0) < ROWS, total - positive, 0.0)
     loss = jnp.sum(loss, axis=0, keepdims=True)
 
+    def unfold(step):
+        chunk = ORDER[step]
+        give.arrived(chunk)
+
+        @pl.loop(0, CROWS // FOLD)
+        def _(g):
+            at = chunk * CROWS + g * FOLD
+            tile = term_landed[pl.ds(at, FOLD)].reshape(FOLDW, FOLDW)
+            flat = matmul(swap[...], tile).astype(BF)
+            for k in range(FOLD):
+                terms[rows_of(at), k * FOLDW : (k + 1) * FOLDW] = flat[k * FOLD : (k + 1) * FOLD]
+
+    unfold(0)
+    unfold(1)
     qs.finish()
     for copy in total_copies:
         copy.wait()
@@ -558,26 +573,12 @@
             sums[...] = got
 
     sum_start(0)
-    for step in range(CHUNKS):
-        chunk = ORDER[step]
-        give.arrived(chunk)
-        lanes = slice(chunk * 128, chunk * 128 + CROWS)
-        names = jnp.where(iota((PAD, CROWS), 0) + 1 == wanted[:, lanes], 1.0, 0.0).astype(BF)
-
-        @pl.loop(0, CROWS // FOLD)
-        def _(g):
-            at = chunk * CROWS + g * FOLD
-            tile = term_landed[pl.ds(at, FOLD)].reshape(FOLDW, FOLDW)
-            flat = matmul(swap[...], tile).astype(BF)
-            for k in range(FOLD):
-                terms[rows_of(at), k * FOLDW : (k + 1) * FOLDW] = flat[k * FOLD : (k + 1) * FOLD]
-
-        if step == 1:
-            sum_end(0)
-            sum_start(1)
-        if step == 2:
-            sum_end(1)
-            sum_start(2)
+    unfold(2)
+    sum_end(0)
+    sum_start(1)
+    unfold(3)
+    sum_end(1)
+    sum_start(2)
 
     names = [
         jnp.where(iota((PAD, CROWS), 0) + 1 == wanted[:, c * 128 : c * 128 + CROWS], 1.0, 0.0).astype(BF)

time: 195 us -> 207 us (1.062)
  Pallas kernels: 181 us -> 193 us
    pallas_call x1, Pallas kernels: 181 us -> 193 us  [local(): pl.pallas_call(kernel, out_shape=(jax.ShapeDtypeStruct((ROWS, WIDTH), F32...]
where the time goes in v3:
time: 207 us; the launch traced here: 206 us
  Pallas kernels  193 us (93%)
  local copies, waits for them, and re-layouts  9.92 us (5%)
  between operations  2.43 us (1%)
    pallas_call x1, Pallas kernels, local(): pl.pallas_call(kernel, out_shape=(jax.ShapeDtypeStruct((ROWS, WIDTH), F32...  193 us
    unnamed x6, local copies, waits for them, and re-layouts  6.24 us

profile of v3, /device:TPU:1, one launch (start us, length us, event | category | flops | bytes accessed | tf_op | source)
XLA Modules:
  0.0 206.3 jit_solution(17913731323298557153)
XLA Ops:
  0.6 1.4 copy.9.owner
  2.0 1.4 copy.10.row_asked
  3.4 0.0 slice-start
  3.4 0.0 slice-start.1
  3.4 0.0 slice-start.2
  3.4 0.0 slice-start.3
  3.4 0.8 slice-done
  4.2 0.2 slice-done.1
  4.5 0.0 slice-done.2
  4.5 0.2 slice-done.3
  4.7 1.1 pad_maximum_fusion.both
  5.7 192.8 %shard_map.84 = (f32[72,4096]{1,0:T(8,128)}, f32[72,4096]{1,0:T(8,128)}, f32[1,4224]{1,0:T(1,128)}) custom-call(bf16[144,4096]{1,0:T(8,128)(2,1)} %pad_maximum_fusion.both, f32[1,4096]{1,0:T(1,128)} %bitcast.3, s32[72,4]{1,0:T(8,128)} %copy.9.owner, s32[72,4]{1,0:T(8,128)} %copy.10.row_asked), custom_call_target="tpu_custom_call" | custom-call | tf_op jit(solution)/shard_map/pallas_call | solution.py:613
  198.6 1.1 slice.23
  200.4 1.3 slice.22
  201.7 0.0 copy-start
  201.7 2.5 %copy.13 = f32[72,4096]{1,0:T(8,128)} copy(f32[72,4096]{1,0:T(8,128)} %get-tuple-element.14) | data formatting | bytes 2359296
  204.1 0.0 copy-done
  204.1 1.0 copy.14
Async XLA Ops:
  3.4 0.8 slice-start
  3.4 1.1 slice-start.1
  3.4 1.1 slice-start.2
  3.4 1.3 slice-start.3
  201.7 2.5 %copy-start = (f32[72,4096]{1,0:T(8,128)S(1)}, f32[72,4096]{1,0:T(8,128)}, u32[]{:S(2)}) copy-start(f32[72,4096]{1,0:T(8,128)} %get-tuple-element.15) | copy-start | bytes 3538948
